TPU v7x, 512 devices: a whole 4x4x16 slice. The times are simulated.
512 devices in a mesh: mesh: 32 (over z, core), run: 16 (over y, x).
Axes of the slice: x: 4, y: 4, z: 16, core: 2. Of those that a mesh axis runs over, the one named last changes fastest.
Arguments:
- snapshots: bfloat16 [65536, 2048], P('mesh', 'run'), may hold values from -6 to 6
- block_cols: int32 [1024, 16], P('mesh'), may hold values from 0 to 1023, as said below
- mass_blocks: bfloat16 [1024, 64, 1024], P('mesh'), as said below
Outputs:
- gram: float32 [2048, 2048], P('mesh', 'run')
Inputs may be any that keep to these rules, and one draw needn't show every extreme that they name: `block_cols`: block row b names 16 different block columns, the first of them b itself; all lie from 2 blocks before the first block row of shard b // 32 to 2 blocks after its last. In every shard but the first, its first block row names the block 2 before the shard; in every shard but the last, its last block row names the block 2 after it. `mass_blocks`: entry [b, i, k * 64 + j] is row i, column j of the k-th stored block of block row b, in the order of block_cols.
All inputs are finite; a program needn't handle non-finite values.
Results may differ from a plain program's by a relative error of at most 0.00056.
Values may be sent and summed in bfloat16 or wider, within the bound.
A program may use at most 64 MiB of HBM per device.

v0:
```python
import jax
import jax.numpy as jnp
from jax import lax
from jax.sharding import PartitionSpec as P

BLK = 64
HB = 2


def extended(block, sides, width):
    for axis, dim in sides:
        count = lax.axis_size(axis)
        forward = [(i, i + 1) for i in range(count - 1)]
        backward = [(target, source) for source, target in forward]
        low = lax.ppermute(
            lax.slice_in_dim(block, block.shape[dim] - width, None, axis=dim), axis, forward
        )
        high = lax.ppermute(lax.slice_in_dim(block, 0, width, axis=dim), axis, backward)
        block = jnp.concatenate([low, block, high], axis=dim)
    return block


def contract_nodes(left_cols, right_cols):
    return lax.dot_general(
        left_cols, right_cols, (((0,), (0,)), ((), ())), preferred_element_type=jnp.float32
    )


def on_device(snapshots, block_cols, mass_blocks):
    node_count = snapshots.shape[0]
    column_count = snapshots.shape[1]
    blocks_here = node_count // BLK
    stored_count = block_cols.shape[1]
    rim_width = HB * BLK
    padded = extended(snapshots, (("mesh", 0),), rim_width)
    shard_index = lax.axis_index("mesh")
    local_cols = block_cols - (shard_index * blocks_here - HB)
    blocked = padded.reshape(blocks_here + 2 * HB, BLK, column_count)
    picked = blocked[local_cols].reshape(blocks_here, stored_count * BLK, column_count)
    weighted = jnp.einsum("bim,bmc->bic", mass_blocks, picked, preferred_element_type=jnp.float32)
    weighted = weighted.astype(jnp.bfloat16).reshape(node_count, column_count)
    gathered = lax.all_gather(snapshots, "run", axis=1, tiled=True)
    partial_term = contract_nodes(gathered, weighted)
    gram = lax.psum_scatter(partial_term, "mesh", scatter_dimension=0, tiled=True)
    return gram


def solution(mesh):
    placed = (P("mesh", "run"), P("mesh", None), P("mesh", None, None))
    return jax.shard_map(
        on_device, mesh=mesh, in_specs=placed, out_specs=P("mesh", "run"), check_vma=False
    )
```

profile of v0, /device:TPU:2, one launch (start us, length us, event | category | flops | bytes accessed | tf_op | source)
XLA Modules:
  0.0 229.1 jit_solution(6387576160055392372)
XLA Ops:
  6.5 0.0 all-gather.2.cloned.1.call-start
  6.5 0.7 all-gather.2.cloned.1.call-update
  7.3 0.0 reduce-scatter.4.cloned.1.call-start
  7.3 0.8 fusion
  8.1 1.7 collective-permute-start
  9.8 1.3 collective-permute-start.1
  11.1 0.7 compare_select_fusion
  11.8 0.1 copy.7
  11.9 0.1 reshape.14
  12.0 0.0 collective-permute-done
  12.0 2.6 %collective-permute-done.1 = bf16[128,128]{1,0:T(8,128)(2,1)S(1)} collective-permute-done((bf16[128,128]{1,0:T(8,128)(2,1)S(1)}, bf16[128,128]{1,0:T(8,128)(2,1)S(1)}, u32[]{:S(2)}, u32[]{:S(2)}) %collective-permute-start.1) | collective-permute-done | bytes 32800 | tf_op jit(solution)/shard_map/ppermute | solution.py:18
  14.6 1.1 pad_maximum_fusion
  15.7 13.4 %gather_fusion = bf16[512,64,128]{2,1,0:T(8,128)(2,1)} fusion(bf16[36,64,128]{2,1,0:T(8,128)(2,1)S(1)} %bitcast.12, s32[1024]{0:T(1024)S(1)} %pad_clamp_fusion), kind=kCustom, calls=%fused_computation | custom fusion | bytes 16779264 | tf_op jit(solution)/shard_map/gather | solution.py:39
  29.1 6.6 %convolution_convert_fusion = bf16[32,128,64]{1,2,0:T(8,128)(2,1)S(1)} fusion(bf16[32,64,1024]{2,1,0:T(8,128)(2,1)} %param.5, bf16[32,1024,128]{2,1,0:T(8,128)(2,1)} %bitcast.13), kind=kOutput, calls=%fused_computation.2 | convolution fusion | flops 537133056 | bytes 13107200 | tf_op jit(solution)/shard_map/bim,bmc->bic/dot_general | solution.py:40
  35.8 72.4 %all-gather.2.cloned.1.call-done = bf16[2048,2048]{1,0:T(8,128)(2,1)} async-done(((bf16[2048,128]{1,0:T(8,128)(2,1)}), bf16[2048,2048]{1,0:T(8,128)(2,1)}) %all-gather.2.cloned.1.call-update) | async-done | bytes 8388624 | tf_op jit(solution)/shard_map/all_gather | solution.py:42
  108.2 4.7 %convolution_bitcast_fusion = f32[2048,128]{0,1:T(8,128)S(1)} fusion(bf16[2048,128]{1,0:T(8,128)(2,1)S(1)} %bitcast.14, bf16[2048,2048]{1,0:T(8,128)(2,1)} %all-gather.2.cloned.1.call-done), kind=kOutput, calls=%fused_computation.1 | convolution fusion | flops 1073741824 | bytes 9961472 | tf_op jit(solution)/shard_map/dot_general | solution.py:24
  112.9 1.3 copy.9
  114.2 0.0 reduce-scatter.4.cloned.1.call-update
  114.2 108.1 %reduce-scatter.4.cloned.1.call-done = f32[64,128]{1,0:T(8,128)} async-done(((f32[2048,128]{1,0:T(8,128)}), f32[64,128]{1,0:T(8,128)}) %reduce-scatter.4.cloned.1.call-update) | async-done | bytes 32784 | tf_op jit(solution)/shard_map/reduce_scatter | solution.py:44
  (1 shorter events, 0.0 us)
Async XLA Ops:
  6.5 101.7 %all-gather.2.cloned.1.call-start = ((), (), s32[]{:S(2)}) async-start(), calls=%async_computation.1 | async-start | bytes 8912896 | tf_op jit(solution)/shard_map/all_gather | solution.py:42
  7.3 215.0 %reduce-scatter.4.cloned.1.call-start = ((), (), s32[]{:S(2)}) async-start(), calls=%async_computation.2 | async-start | bytes 1081344 | tf_op jit(solution)/shard_map/reduce_scatter | solution.py:44
  8.1 3.9 %collective-permute-start = (bf16[128,128]{1,0:T(8,128)(2,1)S(1)}, bf16[128,128]{1,0:T(8,128)(2,1)S(1)}, u32[]{:S(2)}, u32[]{:S(2)}) collective-permute-start(bf16[128,128]{1,0:T(8,128)(2,1)S(1)} %get-tuple-element.5), channel_id=1, source_target_pairs={{0,16},{16,32},{32,48},{48,64},{64,80},{80,96},{96,112},{112,128},... | collective-permute-start | bytes 98312 | tf_op jit(solution)/shard_map/ppermute | solution.py:15
  9.8 4.8 %collective-permute-start.1 = (bf16[128,128]{1,0:T(8,128)(2,1)S(1)}, bf16[128,128]{1,0:T(8,128)(2,1)S(1)}, u32[]{:S(2)}, u32[]{:S(2)}) collective-permute-start(bf16[128,128]{1,0:T(8,128)(2,1)S(1)} %get-tuple-element.6), channel_id=1, source_target_pairs={{16,0},{32,16},{48,32},{64,48},{80,64},{96,80},{112,96},{128,112},... | collective-permute-start | bytes 98312 | tf_op jit(solution)/shard_map/ppermute | solution.py:18
Sparse Core Ops, SparseCore 0:
  10.3 97.8 all-gather.1
  114.3 107.9 reduce-scatter.3
where the time goes:
time: 229 us
  waiting for transfers between devices  184 us (80%)
  local copies, waits for them, and re-layouts  15.7 us (7%)
  between operations  13.4 us (6%)
  matrix products  11.3 us (5%)
  starting transfers between devices  3.06 us (1%)
    reduce_scatter x1, waiting for transfers between devices, on_device(): lax.psum_scatter(partial_term, 'mesh', scatter_dimension=0, tiled=True)  108 us
    all_gather x1, waiting for transfers between devices, on_device(): gathered = lax.all_gather(snapshots, 'run', axis=1, tiled=True)  72.4 us
    gather x1, local copies, waits for them, and re-layouts, on_device(): blocked[local_cols].reshape(blocks_here, stored_count * BLK, column_count)  13.4 us
    dot_general x1, matrix products, on_device(): jnp.einsum('bim,bmc->bic', mass_blocks, picked, preferred_element_type=jn...  6.61 us
    dot_general x1, matrix products, contract_nodes(): lax.dot_general(left_cols, right_cols, (((0,), (0,)), ((), ())), preferre...  4.66 us
  transfers between devices with their start and end apart: 4, of which 3 were waited for; matrix products, arithmetic and copies ran while one was open for 10% of the time, Pallas kernels for 0%

commit v1 on v0

--- a/solution.py
+++ b/solution.py
@@ -5,6 +5,12 @@
 
 BLK = 64
 HB = 2
+
+
+def joined_along(pieces, dim):
+    pieces = jnp.moveaxis(pieces, 0, dim)
+    dims = pieces.shape
+    return pieces.reshape(*dims[:dim], dims[dim] * dims[dim + 1], *dims[dim + 2 :])
 
 
 def extended(block, sides, width):
@@ -39,7 +45,19 @@
     picked = blocked[local_cols].reshape(blocks_here, stored_count * BLK, column_count)
     weighted = jnp.einsum("bim,bmc->bic", mass_blocks, picked, preferred_element_type=jnp.float32)
     weighted = weighted.astype(jnp.bfloat16).reshape(node_count, column_count)
-    gathered = lax.all_gather(snapshots, "run", axis=1, tiled=True)
+    count_2 = lax.axis_size("run")
+    pairs = [(i_2, (i_2 + 1) % count_2) for i_2 in range(count_2)]
+    back = [(b, a) for a, b in pairs]
+    lower, upper = ([], [])
+    for step in range(count_2 - 1):
+        if step % 2 == 0:
+            lower.append(lax.ppermute(lower[-1] if lower else snapshots, "run", pairs))
+        else:
+            upper.append(lax.ppermute(upper[-1] if upper else snapshots, "run", back))
+    blocks = jnp.stack([*lower[::-1], snapshots, *upper])
+    shift = lax.axis_index("run") - len(lower)
+    blocks = blocks[(jnp.arange(count_2) - shift) % count_2]
+    gathered = joined_along(blocks, 1)
     partial_term = contract_nodes(gathered, weighted)
     gram = lax.psum_scatter(partial_term, "mesh", scatter_dimension=0, tiled=True)
     return gram

time: 229 us -> 313 us (1.37)
  starting transfers between devices: 3.06 us -> 67.4 us
  local copies, waits for them, and re-layouts: 15.7 us -> 53.5 us
  waiting for transfers between devices: 184 us -> 162 us
    all_gather x1 -> x0, waiting for transfers between devices: 72.4 us -> none  [on_device(): gathered = lax.all_gather(snapshots, 'run', axis=1, tiled=True)]
    ppermute x0 -> x15, starting transfers between devices: none -> 64.8 us  [the longest x7 39.5 us: on_device(): upper.append(lax.ppermute(upper[-1] if upper else snapshots, 'run', back))]
    ppermute x0 -> x15, waiting for transfers between devices: none -> 37.7 us  [the longest x8 35.2 us: on_device(): lower.append(lax.ppermute(lower[-1] if lower else snapshots, 'run', pairs))]
    unnamed x1 -> x25, local copies, waits for them, and re-layouts: 1.31 us -> 17.7 us
    reduce_scatter x1, waiting for transfers between devices: 108 us -> 124 us  [on_device(): lax.psum_scatter(partial_term, 'mesh', scatter_dimension=0, tiled=True)]
    transpose x0 -> x1, local copies, waits for them, and re-layouts: none -> 12.4 us  [joined_along(): pieces = jnp.moveaxis(pieces, 0, dim)]
    gather x0 -> x1, local copies, waits for them, and re-layouts: none -> 8.14 us  [on_device(): blocks = blocks[(jnp.arange(count_2) - shift) % count_2]]
  transfers between devices with their start and end apart: 4 -> 18, of which waited for: 3 -> 10; matrix products, arithmetic and copies ran while one was open for 10% -> 13% of each run, Pallas kernels for 0% -> 0%
where the time goes in v1:
time: 313 us; the launch traced here: 312 us
  waiting for transfers between devices  162 us (52%)
  starting transfers between devices  67.4 us (22%)
  local copies, waits for them, and re-layouts  53.5 us (17%)
  between operations  13.6 us (4%)
  matrix products  13 us (4%)
    reduce_scatter x1, waiting for transfers between devices, on_device(): lax.psum_scatter(partial_term, 'mesh', scatter_dimension=0, tiled=True)  124 us
    ppermute x7, starting transfers between devices, on_device(): upper.append(lax.ppermute(upper[-1] if upper else snapshots, 'run', back))  39.5 us
    ppermute x8, waiting for transfers between devices, on_device(): lower.append(lax.ppermute(lower[-1] if lower else snapshots, 'run', pairs))  35.2 us
    ppermute x8, starting transfers between devices, on_device(): lower.append(lax.ppermute(lower[-1] if lower else snapshots, 'run', pairs))  25.3 us
    unnamed x25, local copies, waits for them, and re-layouts  17.7 us
    gather x1, local copies, waits for them, and re-layouts, on_device(): blocked[local_cols].reshape(blocks_here, stored_count * BLK, column_count)  13.5 us
    transpose x1, local copies, waits for them, and re-layouts, joined_along(): pieces = jnp.moveaxis(pieces, 0, dim)  12.4 us
    gather x1, local copies, waits for them, and re-layouts, on_device(): blocks = blocks[(jnp.arange(count_2) - shift) % count_2]  8.14 us
  transfers between devices with their start and end apart: 18, of which 10 were waited for; matrix products, arithmetic and copies ran while one was open for 13% of the time, Pallas kernels for 0%

profile of v1, /device:TPU:2, one launch (start us, length us, event | category | flops | bytes accessed | tf_op | source)
XLA Modules:
  0.0 311.7 jit_solution(17677241988359092098)
XLA Ops:
  6.5 3.4 %collective-permute-start = (bf16[2048,128]{1,0:T(8,128)(2,1)}, bf16[2048,128]{1,0:T(8,128)(2,1)S(1)}, u32[]{:S(2)}, u32[]{:S(2)}) collective-permute-start(bf16[2048,128]{1,0:T(8,128)(2,1)} %param.3), channel_id=1, source_target_pairs={{0,1},{1,2},{2,3},{3,4},{4,5},{5,6},{6,7},{7,8},{8,9},{9,10},{10,1... | collective-permute-start | bytes 1572872 | tf_op jit(solution)/shard_map/ppermute | solution.py:54
  9.9 12.4 %collective-permute-done = bf16[2048,128]{1,0:T(8,128)(2,1)S(1)} collective-permute-done((bf16[2048,128]{1,0:T(8,128)(2,1)}, bf16[2048,128]{1,0:T(8,128)(2,1)S(1)}, u32[]{:S(2)}, u32[]{:S(2)}) %collective-permute-start) | collective-permute-done | bytes 524320 | tf_op jit(solution)/shard_map/ppermute | solution.py:54
  22.3 3.4 %collective-permute-start.1 = (bf16[2048,128]{1,0:T(8,128)(2,1)S(1)}, bf16[2048,128]{1,0:T(8,128)(2,1)S(1)}, u32[]{:S(2)}, u32[]{:S(2)}) collective-permute-start(bf16[2048,128]{1,0:T(8,128)(2,1)S(1)} %collective-permute-done), channel_id=1, source_target_pairs={{0,1},{1,2},{2,3},{3,4},{4,5},{5,6},{6,7},{7,8},{8,9},{9,10},{10,1... | collective-permute-start | bytes 1572872 | tf_op jit(solution)/shard_map/ppermute | solution.py:54
  25.7 5.2 %collective-permute-start.8 = (bf16[2048,128]{1,0:T(8,128)(2,1)}, bf16[2048,128]{1,0:T(8,128)(2,1)S(1)}, u32[]{:S(2)}, u32[]{:S(2)}) collective-permute-start(bf16[2048,128]{1,0:T(8,128)(2,1)} %param.3), channel_id=1, source_target_pairs={{1,0},{2,1},{3,2},{4,3},{5,4},{6,5},{7,6},{8,7},{9,8},{10,9},{11,1... | collective-permute-start | bytes 1572872 | tf_op jit(solution)/shard_map/ppermute | solution.py:56
  30.9 5.2 %collective-permute-done.1 = bf16[2048,128]{1,0:T(8,128)(2,1)S(1)} collective-permute-done((bf16[2048,128]{1,0:T(8,128)(2,1)S(1)}, bf16[2048,128]{1,0:T(8,128)(2,1)S(1)}, u32[]{:S(2)}, u32[]{:S(2)}) %collective-permute-start.1) | collective-permute-done | bytes 524320 | tf_op jit(solution)/shard_map/ppermute | solution.py:54
  36.1 4.3 %collective-permute-start.2 = (bf16[2048,128]{1,0:T(8,128)(2,1)S(1)}, bf16[2048,128]{1,0:T(8,128)(2,1)S(1)}, u32[]{:S(2)}, u32[]{:S(2)}) collective-permute-start(bf16[2048,128]{1,0:T(8,128)(2,1)S(1)} %collective-permute-done.1), channel_id=1, source_target_pairs={{0,1},{1,2},{2,3},{3,4},{4,5},{5,6},{6,7},{7,8},{8,9},{9,10},{10,1... | collective-permute-start | bytes 1572872 | tf_op jit(solution)/shard_map/ppermute | solution.py:54
  40.4 4.9 %collective-permute-start.9 = (bf16[2048,128]{1,0:T(8,128)(2,1)S(1)}, bf16[2048,128]{1,0:T(8,128)(2,1)S(1)}, u32[]{:S(2)}, u32[]{:S(2)}) collective-permute-start(bf16[2048,128]{1,0:T(8,128)(2,1)S(1)} %collective-permute-done.8), channel_id=1, source_target_pairs={{1,0},{2,1},{3,2},{4,3},{5,4},{6,5},{7,6},{8,7},{9,8},{10,9},{11,1... | collective-permute-start | bytes 1572872 | tf_op jit(solution)/shard_map/ppermute | solution.py:56
  45.3 5.2 %collective-permute-done.2 = bf16[2048,128]{1,0:T(8,128)(2,1)S(1)} collective-permute-done((bf16[2048,128]{1,0:T(8,128)(2,1)S(1)}, bf16[2048,128]{1,0:T(8,128)(2,1)S(1)}, u32[]{:S(2)}, u32[]{:S(2)}) %collective-permute-start.2) | collective-permute-done | bytes 524320 | tf_op jit(solution)/shard_map/ppermute | solution.py:54
  50.5 3.6 %collective-permute-start.3 = (bf16[2048,128]{1,0:T(8,128)(2,1)S(1)}, bf16[2048,128]{1,0:T(8,128)(2,1)S(1)}, u32[]{:S(2)}, u32[]{:S(2)}) collective-permute-start(bf16[2048,128]{1,0:T(8,128)(2,1)S(1)} %collective-permute-done.2), channel_id=1, source_target_pairs={{0,1},{1,2},{2,3},{3,4},{4,5},{5,6},{6,7},{7,8},{8,9},{9,10},{10,1... | collective-permute-start | bytes 1572872 | tf_op jit(solution)/shard_map/ppermute | solution.py:54
  55.4 4.3 %collective-permute-start.10 = (bf16[2048,128]{1,0:T(8,128)(2,1)S(1)}, bf16[2048,128]{1,0:T(8,128)(2,1)S(1)}, u32[]{:S(2)}, u32[]{:S(2)}) collective-permute-start(bf16[2048,128]{1,0:T(8,128)(2,1)S(1)} %collective-permute-done.9), channel_id=1, source_target_pairs={{1,0},{2,1},{3,2},{4,3},{5,4},{6,5},{7,6},{8,7},{9,8},{10,9},{11,1... | collective-permute-start | bytes 1572872 | tf_op jit(solution)/shard_map/ppermute | solution.py:56
  59.7 5.2 %collective-permute-done.3 = bf16[2048,128]{1,0:T(8,128)(2,1)S(1)} collective-permute-done((bf16[2048,128]{1,0:T(8,128)(2,1)S(1)}, bf16[2048,128]{1,0:T(8,128)(2,1)S(1)}, u32[]{:S(2)}, u32[]{:S(2)}) %collective-permute-start.3) | collective-permute-done | bytes 524320 | tf_op jit(solution)/shard_map/ppermute | solution.py:54
  64.9 4.0 %collective-permute-start.4 = (bf16[2048,128]{1,0:T(8,128)(2,1)S(1)}, bf16[2048,128]{1,0:T(8,128)(2,1)}, u32[]{:S(2)}, u32[]{:S(2)}) collective-permute-start(bf16[2048,128]{1,0:T(8,128)(2,1)S(1)} %collective-permute-done.3), channel_id=1, source_target_pairs={{0,1},{1,2},{2,3},{3,4},{4,5},{5,6},{6,7},{7,8},{8,9},{9,10},{10,1... | collective-permute-start | bytes 1572872 | tf_op jit(solution)/shard_map/ppermute | solution.py:54
  70.1 4.2 %collective-permute-start.11 = (bf16[2048,128]{1,0:T(8,128)(2,1)S(1)}, bf16[2048,128]{1,0:T(8,128)(2,1)}, u32[]{:S(2)}, u32[]{:S(2)}) collective-permute-start(bf16[2048,128]{1,0:T(8,128)(2,1)S(1)} %collective-permute-done.10), channel_id=1, source_target_pairs={{1,0},{2,1},{3,2},{4,3},{5,4},{6,5},{7,6},{8,7},{9,8},{10,9},{11,1... | collective-permute-start | bytes 1572872 | tf_op jit(solution)/shard_map/ppermute | solution.py:56
  74.4 5.8 %collective-permute-done.4 = bf16[2048,128]{1,0:T(8,128)(2,1)} collective-permute-done((bf16[2048,128]{1,0:T(8,128)(2,1)S(1)}, bf16[2048,128]{1,0:T(8,128)(2,1)}, u32[]{:S(2)}, u32[]{:S(2)}) %collective-permute-start.4) | collective-permute-done | bytes 524320 | tf_op jit(solution)/shard_map/ppermute | solution.py:54
  80.1 2.8 collective-permute-start.5
  87.0 6.7 %collective-permute-start.12 = (bf16[2048,128]{1,0:T(8,128)(2,1)}, bf16[2048,128]{1,0:T(8,128)(2,1)}, u32[]{:S(2)}, u32[]{:S(2)}) collective-permute-start(bf16[2048,128]{1,0:T(8,128)(2,1)} %collective-permute-done.11), channel_id=1, source_target_pairs={{1,0},{2,1},{3,2},{4,3},{5,4},{6,5},{7,6},{8,7},{9,8},{10,9},{11,1... | collective-permute-start | bytes 1572872 | tf_op jit(solution)/shard_map/ppermute | solution.py:56
  98.8 13.5 %gather_fusion.1 = bf16[512,64,128]{2,1,0:T(8,128)(2,1)} fusion(bf16[36,64,128]{2,1,0:T(8,128)(2,1)S(1)} %bitcast.45, s32[1024]{0:T(1024)S(1)} %pad_clamp_fusion), kind=kCustom, calls=%fused_computation.1 | custom fusion | bytes 16779264 | tf_op jit(solution)/shard_map/gather | solution.py:45
  112.3 7.0 %collective-permute-start.13 = (bf16[2048,128]{1,0:T(8,128)(2,1)}, bf16[2048,128]{1,0:T(8,128)(2,1)S(1)}, u32[]{:S(2)}, u32[]{:S(2)}) collective-permute-start(bf16[2048,128]{1,0:T(8,128)(2,1)} %collective-permute-done.12), channel_id=1, source_target_pairs={{1,0},{2,1},{3,2},{4,3},{5,4},{6,5},{7,6},{8,7},{9,8},{10,9},{11,1... | collective-permute-start | bytes 1572872 | tf_op jit(solution)/shard_map/ppermute | solution.py:56
  121.2 6.3 %convolution_convert_fusion = bf16[32,128,64]{1,2,0:T(8,128)(2,1)S(1)} fusion(bf16[32,64,1024]{2,1,0:T(8,128)(2,1)} %param.5, bf16[32,1024,128]{2,1,0:T(8,128)(2,1)} %bitcast.46), kind=kOutput, calls=%fused_computation.2 | convolution fusion | flops 537133056 | bytes 13107200 | tf_op jit(solution)/shard_map/bim,bmc->bic/dot_general | solution.py:46
  127.5 7.4 %collective-permute-start.14 = (bf16[2048,128]{1,0:T(8,128)(2,1)S(1)}, bf16[2048,128]{1,0:T(8,128)(2,1)S(1)}, u32[]{:S(2)}, u32[]{:S(2)}) collective-permute-start(bf16[2048,128]{1,0:T(8,128)(2,1)S(1)} %collective-permute-done.13), channel_id=1, source_target_pairs={{1,0},{2,1},{3,2},{4,3},{5,4},{6,5},{7,6},{8,7},{9,8},{10,9},{11,1... | collective-permute-start | bytes 1572872 | tf_op jit(solution)/shard_map/ppermute | solution.py:56
  153.5 8.1 %gather_fusion = bf16[16,2048,128]{2,1,0:T(8,128)(2,1)} fusion(bf16[16,2048,128]{2,1,0:T(8,128)(2,1)} %bitcast_dynamic-update-slice_fusion, s32[1024]{0:T(1024)S(1)} %pad_clamp_fusion.1), kind=kCustom, calls=%fused_computation | custom fusion | bytes 16777280 | tf_op jit(solution)/shard_map/gather | solution.py:59
  161.6 12.4 %copy.5 = bf16[2048,16,128]{0,2,1:T(8,128)(2,1)} copy(bf16[2048,16,128]{2,0,1:T(8,128)(2,1)} %bitcast.47) | data formatting | bytes 16777216 | tf_op jit(solution)/shard_map/transpose | solution.py:11
  174.0 6.8 %fusion.3 = f32[2048,128]{1,0:T(8,128)} fusion(bf16[2048,2048]{0,1:T(8,128)(2,1)} %bitcast.48, bf16[2048,128]{1,0:T(8,128)(2,1)S(1)} %bitcast.49), kind=kOutput, calls=%fused_computation.30 | convolution fusion | flops 1073741824 | bytes 9961472 | tf_op jit(solution)/shard_map/dot_general | solution.py:30
  180.8 124.1 %reduce-scatter.2.cloned.1.call-done = f32[64,128]{1,0:T(8,128)} async-done(((f32[2048,128]{1,0:T(8,128)}), f32[64,128]{1,0:T(8,128)}) %reduce-scatter.2.cloned.1.call-update) | async-done | bytes 32784 | tf_op jit(solution)/shard_map/reduce_scatter | solution.py:62
  (52 shorter events, 32.2 us)
Async XLA Ops:
  6.5 298.3 %reduce-scatter.2.cloned.1.call-start = ((), (), s32[]{:S(2)}) async-start(), calls=%async_computation.1 | async-start | bytes 1081344 | tf_op jit(solution)/shard_map/reduce_scatter | solution.py:62
  6.5 15.8 %collective-permute-start = (bf16[2048,128]{1,0:T(8,128)(2,1)}, bf16[2048,128]{1,0:T(8,128)(2,1)S(1)}, u32[]{:S(2)}, u32[]{:S(2)}) collective-permute-start(bf16[2048,128]{1,0:T(8,128)(2,1)} %param.3), channel_id=1, source_target_pairs={{0,1},{1,2},{2,3},{3,4},{4,5},{5,6},{6,7},{7,8},{8,9},{9,10},{10,1... | collective-permute-start | bytes 1572872 | tf_op jit(solution)/shard_map/ppermute | solution.py:54
  22.3 13.8 %collective-permute-start.1 = (bf16[2048,128]{1,0:T(8,128)(2,1)S(1)}, bf16[2048,128]{1,0:T(8,128)(2,1)S(1)}, u32[]{:S(2)}, u32[]{:S(2)}) collective-permute-start(bf16[2048,128]{1,0:T(8,128)(2,1)S(1)} %collective-permute-done), channel_id=1, source_target_pairs={{0,1},{1,2},{2,3},{3,4},{4,5},{5,6},{6,7},{7,8},{8,9},{9,10},{10,1... | collective-permute-start | bytes 1572872 | tf_op jit(solution)/shard_map/ppermute | solution.py:54
  25.7 14.7 %collective-permute-start.8 = (bf16[2048,128]{1,0:T(8,128)(2,1)}, bf16[2048,128]{1,0:T(8,128)(2,1)S(1)}, u32[]{:S(2)}, u32[]{:S(2)}) collective-permute-start(bf16[2048,128]{1,0:T(8,128)(2,1)} %param.3), channel_id=1, source_target_pairs={{1,0},{2,1},{3,2},{4,3},{5,4},{6,5},{7,6},{8,7},{9,8},{10,9},{11,1... | collective-permute-start | bytes 1572872 | tf_op jit(solution)/shard_map/ppermute | solution.py:56
  36.1 14.4 %collective-permute-start.2 = (bf16[2048,128]{1,0:T(8,128)(2,1)S(1)}, bf16[2048,128]{1,0:T(8,128)(2,1)S(1)}, u32[]{:S(2)}, u32[]{:S(2)}) collective-permute-start(bf16[2048,128]{1,0:T(8,128)(2,1)S(1)} %collective-permute-done.1), channel_id=1, source_target_pairs={{0,1},{1,2},{2,3},{3,4},{4,5},{5,6},{6,7},{7,8},{8,9},{9,10},{10,1... | collective-permute-start | bytes 1572872 | tf_op jit(solution)/shard_map/ppermute | solution.py:54
  40.4 15.0 %collective-permute-start.9 = (bf16[2048,128]{1,0:T(8,128)(2,1)S(1)}, bf16[2048,128]{1,0:T(8,128)(2,1)S(1)}, u32[]{:S(2)}, u32[]{:S(2)}) collective-permute-start(bf16[2048,128]{1,0:T(8,128)(2,1)S(1)} %collective-permute-done.8), channel_id=1, source_target_pairs={{1,0},{2,1},{3,2},{4,3},{5,4},{6,5},{7,6},{8,7},{9,8},{10,9},{11,1... | collective-permute-start | bytes 1572872 | tf_op jit(solution)/shard_map/ppermute | solution.py:56
  50.5 14.4 %collective-permute-start.3 = (bf16[2048,128]{1,0:T(8,128)(2,1)S(1)}, bf16[2048,128]{1,0:T(8,128)(2,1)S(1)}, u32[]{:S(2)}, u32[]{:S(2)}) collective-permute-start(bf16[2048,128]{1,0:T(8,128)(2,1)S(1)} %collective-permute-done.2), channel_id=1, source_target_pairs={{0,1},{1,2},{2,3},{3,4},{4,5},{5,6},{6,7},{7,8},{8,9},{9,10},{10,1... | collective-permute-start | bytes 1572872 | tf_op jit(solution)/shard_map/ppermute | solution.py:54
  55.4 14.7 %collective-permute-start.10 = (bf16[2048,128]{1,0:T(8,128)(2,1)S(1)}, bf16[2048,128]{1,0:T(8,128)(2,1)S(1)}, u32[]{:S(2)}, u32[]{:S(2)}) collective-permute-start(bf16[2048,128]{1,0:T(8,128)(2,1)S(1)} %collective-permute-done.9), channel_id=1, source_target_pairs={{1,0},{2,1},{3,2},{4,3},{5,4},{6,5},{7,6},{8,7},{9,8},{10,9},{11,1... | collective-permute-start | bytes 1572872 | tf_op jit(solution)/shard_map/ppermute | solution.py:56
  64.9 5.3 %copy-start.3 = (bf16[2048,128]{1,0:T(8,128)(2,1)}, bf16[2048,128]{1,0:T(8,128)(2,1)S(1)}, u32[]{:S(2)}) copy-start(bf16[2048,128]{1,0:T(8,128)(2,1)S(1)} %collective-permute-done.3) | copy-start | bytes 1572868
  64.9 15.3 %collective-permute-start.4 = (bf16[2048,128]{1,0:T(8,128)(2,1)S(1)}, bf16[2048,128]{1,0:T(8,128)(2,1)}, u32[]{:S(2)}, u32[]{:S(2)}) collective-permute-start(bf16[2048,128]{1,0:T(8,128)(2,1)S(1)} %collective-permute-done.3), channel_id=1, source_target_pairs={{0,1},{1,2},{2,3},{3,4},{4,5},{5,6},{6,7},{7,8},{8,9},{9,10},{10,1... | collective-permute-start | bytes 1572872 | tf_op jit(solution)/shard_map/ppermute | solution.py:54
  70.1 27.1 %copy-start.1 = (bf16[2048,128]{1,0:T(8,128)(2,1)}, bf16[2048,128]{1,0:T(8,128)(2,1)S(1)}, u32[]{:S(2)}) copy-start(bf16[2048,128]{1,0:T(8,128)(2,1)S(1)} %collective-permute-done.10) | copy-start | bytes 1572868
  70.1 16.9 %collective-permute-start.11 = (bf16[2048,128]{1,0:T(8,128)(2,1)S(1)}, bf16[2048,128]{1,0:T(8,128)(2,1)}, u32[]{:S(2)}, u32[]{:S(2)}) collective-permute-start(bf16[2048,128]{1,0:T(8,128)(2,1)S(1)} %collective-permute-done.10), channel_id=1, source_target_pairs={{1,0},{2,1},{3,2},{4,3},{5,4},{6,5},{7,6},{8,7},{9,8},{10,9},{11,1... | collective-permute-start | bytes 1572872 | tf_op jit(solution)/shard_map/ppermute | solution.py:56
  80.1 15.0 %collective-permute-start.5 = (bf16[2048,128]{1,0:T(8,128)(2,1)}, bf16[2048,128]{1,0:T(8,128)(2,1)}, u32[]{:S(2)}, u32[]{:S(2)}) collective-permute-start(bf16[2048,128]{1,0:T(8,128)(2,1)} %collective-permute-done.4), channel_id=1, source_target_pairs={{0,1},{1,2},{2,3},{3,4},{4,5},{5,6},{6,7},{7,8},{8,9},{9,10},{10,1... | collective-permute-start | bytes 1572872 | tf_op jit(solution)/shard_map/ppermute | solution.py:54
  83.7 13.5 %collective-permute-start.15 = (bf16[128,128]{1,0:T(8,128)(2,1)S(1)}, bf16[128,128]{1,0:T(8,128)(2,1)S(1)}, u32[]{:S(2)}, u32[]{:S(2)}) collective-permute-start(bf16[128,128]{1,0:T(8,128)(2,1)S(1)} %get-tuple-element.5), channel_id=1, source_target_pairs={{0,16},{16,32},{32,48},{48,64},{64,80},{80,96},{96,112},{112,128},... | collective-permute-start | bytes 98312 | tf_op jit(solution)/shard_map/ppermute | solution.py:21
  85.0 12.8 %collective-permute-start.16 = (bf16[128,128]{1,0:T(8,128)(2,1)S(1)}, bf16[128,128]{1,0:T(8,128)(2,1)S(1)}, u32[]{:S(2)}, u32[]{:S(2)}) collective-permute-start(bf16[128,128]{1,0:T(8,128)(2,1)S(1)} %get-tuple-element.6), channel_id=1, source_target_pairs={{16,0},{32,16},{48,32},{64,48},{80,64},{96,80},{112,96},{128,112},... | collective-permute-start | bytes 98312 | tf_op jit(solution)/shard_map/ppermute | solution.py:24
  87.0 25.3 %collective-permute-start.12 = (bf16[2048,128]{1,0:T(8,128)(2,1)}, bf16[2048,128]{1,0:T(8,128)(2,1)}, u32[]{:S(2)}, u32[]{:S(2)}) collective-permute-start(bf16[2048,128]{1,0:T(8,128)(2,1)} %collective-permute-done.11), channel_id=1, source_target_pairs={{1,0},{2,1},{3,2},{4,3},{5,4},{6,5},{7,6},{8,7},{9,8},{10,9},{11,1... | collective-permute-start | bytes 1572872 | tf_op jit(solution)/shard_map/ppermute | solution.py:56
  95.1 24.2 %collective-permute-start.6 = (bf16[2048,128]{1,0:T(8,128)(2,1)}, bf16[2048,128]{1,0:T(8,128)(2,1)}, u32[]{:S(2)}, u32[]{:S(2)}) collective-permute-start(bf16[2048,128]{1,0:T(8,128)(2,1)} %collective-permute-done.5), channel_id=1, source_target_pairs={{0,1},{1,2},{2,3},{3,4},{4,5},{5,6},{6,7},{7,8},{8,9},{9,10},{10,1... | collective-permute-start | bytes 1572872 | tf_op jit(solution)/shard_map/ppermute | solution.py:54
  112.3 15.2 %collective-permute-start.13 = (bf16[2048,128]{1,0:T(8,128)(2,1)}, bf16[2048,128]{1,0:T(8,128)(2,1)S(1)}, u32[]{:S(2)}, u32[]{:S(2)}) collective-permute-start(bf16[2048,128]{1,0:T(8,128)(2,1)} %collective-permute-done.12), channel_id=1, source_target_pairs={{1,0},{2,1},{3,2},{4,3},{5,4},{6,5},{7,6},{8,7},{9,8},{10,9},{11,1... | collective-permute-start | bytes 1572872 | tf_op jit(solution)/shard_map/ppermute | solution.py:56
  119.3 15.6 %collective-permute-start.7 = (bf16[2048,128]{1,0:T(8,128)(2,1)}, bf16[2048,128]{1,0:T(8,128)(2,1)S(1)}, u32[]{:S(2)}, u32[]{:S(2)}) collective-permute-start(bf16[2048,128]{1,0:T(8,128)(2,1)} %collective-permute-done.6), channel_id=1, source_target_pairs={{0,1},{1,2},{2,3},{3,4},{4,5},{5,6},{6,7},{7,8},{8,9},{9,10},{10,1... | collective-permute-start | bytes 1572872 | tf_op jit(solution)/shard_map/ppermute | solution.py:54
  121.2 20.2 %copy-start.4 = (bf16[2048,128]{1,0:T(8,128)(2,1)S(1)}, bf16[2048,128]{1,0:T(8,128)(2,1)}, u32[]{:S(2)}) copy-start(bf16[2048,128]{1,0:T(8,128)(2,1)} %copy-done.3) | copy-start | bytes 1572868
  127.5 17.2 %copy-start = (bf16[2048,128]{1,0:T(8,128)(2,1)S(1)}, bf16[2048,128]{1,0:T(8,128)(2,1)}, u32[]{:S(2)}) copy-start(bf16[2048,128]{1,0:T(8,128)(2,1)} %param.3) | copy-start | bytes 1572868
  127.5 19.7 %copy-start.2 = (bf16[2048,128]{1,0:T(8,128)(2,1)S(1)}, bf16[2048,128]{1,0:T(8,128)(2,1)}, u32[]{:S(2)}) copy-start(bf16[2048,128]{1,0:T(8,128)(2,1)} %copy-done.1) | copy-start | bytes 1572868
  127.5 25.0 %collective-permute-start.14 = (bf16[2048,128]{1,0:T(8,128)(2,1)S(1)}, bf16[2048,128]{1,0:T(8,128)(2,1)S(1)}, u32[]{:S(2)}, u32[]{:S(2)}) collective-permute-start(bf16[2048,128]{1,0:T(8,128)(2,1)S(1)} %collective-permute-done.13), channel_id=1, source_target_pairs={{1,0},{2,1},{3,2},{4,3},{5,4},{6,5},{7,6},{8,7},{9,8},{10,9},{11,1... | collective-permute-start | bytes 1572872 | tf_op jit(solution)/shard_map/ppermute | solution.py:56
Sparse Core Ops, SparseCore 0:
  180.9 123.8 reduce-scatter.1
